TPU v7x, 512 devices: a whole 4x8x8 slice. The times are simulated.
512 devices in a mesh: load: 32 (over x, y), tm: 16 (over z, core).
Axes of the slice: x: 4, y: 8, z: 8, core: 2. Of those that a mesh axis runs over, the one named last changes fastest.
Arguments:
- frames: bfloat16 [16, 1024, 8, 24, 256], P('tm', 'load'), may hold values from -6 to 6
- counts: int32 [16, 1024], P('tm', 'load'), may hold values from 3 to 8
- dest: int32 [1024], P('load'), may hold values from 0 to 1023, as said below
- first_weight: bfloat16 [3, 256, 256], replicated, may hold values from -0.21875 to 0.21875
- second_weight: bfloat16 [3, 256, 256], replicated, may hold values from -0.21875 to 0.21875
- gain: float32 [256], replicated, may hold values from 0.5 to 2
- bias: float32 [256], replicated, may hold values from -3 to 3
Outputs:
- latents: bfloat16 [16, 1024, 2, 24, 256], P('tm', 'load')
Inputs may be any that keep to these rules, and one draw needn't show every extreme that they name: dest is a permutation; video c goes to owner dest // 32, the load index that holds output rows of that block. A loader sends each owner none or exactly 2 of its videos, and an owner's slots 2 i and 2 i + 1 hold videos of one loader.
All inputs are finite; a program needn't handle non-finite values.
Results may differ from a plain program's by a relative error of at most 0.009.
Values may be sent and summed in bfloat16 or wider, within the bound.
A program may use at most 64 MiB of HBM per device.

v0:
```python
import jax
import jax.numpy as jnp
from jax import lax
from jax.sharding import PartitionSpec as P

CAP = 2


def shifted(value, axis, steps):
    count = lax.axis_size(axis)
    leading, last = (max(0, -steps), min(count, count - steps))
    return lax.ppermute(value, axis, [(source, source + steps) for source in range(leading, last)])


def prefix(part, axis, combine, identity):
    place = lax.axis_index(axis)
    gathered = jax.tree.map(lambda a: lax.all_gather(a, axis), part)
    state = jax.tree.map(lambda a, e: jnp.zeros_like(a) + jnp.asarray(e, a.dtype), part, identity)

    def one(hop, state):
        return combine(
            state, jax.tree.map(lambda a: lax.dynamic_index_in_dim(a, hop, 0, False), gathered)
        )

    return lax.fori_loop(0, place, one, state)


def last_two(block, count):
    index = (count[:, None] - 2 + jnp.arange(2, dtype=jnp.int32)[None, :]).astype(jnp.int32)
    return jnp.take_along_axis(block, index[:, :, None, None], axis=1)


def causal_layer(block, context, weight):
    extended = jnp.concatenate([context, block], axis=1)
    outlen = block.shape[1] // 2
    total = jnp.zeros((block.shape[0], outlen, block.shape[2], weight.shape[2]), jnp.float32)
    for tap in range(3):
        taken = extended[:, tap : tap + 2 * outlen - 1 : 2]
        total = total + jnp.einsum(
            "kjpc,cd->kjpd", taken, weight[tap], preferred_element_type=jnp.float32
        )
    return total


def live_mask(count, length, step):
    return (step * jnp.arange(length, dtype=jnp.int32)[None, :] < count[:, None])[:, :, None, None]


def first_section(block, context, count, weight):
    first = jax.nn.silu(causal_layer(block, context, weight))
    return jnp.where(live_mask(count, block.shape[1] // 2, 2), first, 0.0).astype(jnp.bfloat16)


def add_stats(earlier, later):
    return (earlier[0] + later[0], earlier[1] + later[1], earlier[2] + later[2])


def body(frames, counts, dest, first_weight, second_weight, gain, bias):
    block = frames[0]
    count = counts[0]
    slots = block.shape[0]
    places = block.shape[2]
    loads = lax.axis_size("load")
    width = loads * CAP
    block = jnp.where(live_mask(count, block.shape[1], 1), block, jnp.zeros_like(block))
    owners = dest // slots
    order = jnp.arange(slots, dtype=jnp.int32)
    before = (owners[:, None] == owners[None, :]) & (order[None, :] < order[:, None])
    place = owners * CAP + jnp.sum(before.astype(jnp.int32), axis=1)
    hits = place[None, :] == jnp.arange(width, dtype=jnp.int32)[:, None]
    source = jnp.sum(hits.astype(jnp.int32) * order[None, :], axis=1)
    filled = jnp.any(hits, axis=1)
    send_count = jnp.where(filled, jnp.take(count, source), 0).reshape(loads, CAP)
    send_slot = jnp.where(filled, jnp.take(dest % slots, source), -1).reshape(loads, CAP)
    taken = jnp.take(block, source, axis=0)
    taken = jnp.where(filled[:, None, None, None], taken, jnp.zeros_like(taken))
    received = lax.all_to_all(
        taken.reshape((loads, CAP) + block.shape[1:]),
        "load",
        split_axis=0,
        concat_axis=0,
        tiled=True,
    )
    received_count = lax.all_to_all(send_count, "load", split_axis=0, concat_axis=0, tiled=True)
    received_slot = lax.all_to_all(send_slot, "load", split_axis=0, concat_axis=0, tiled=True)
    flat_slot = received_slot.reshape(-1)
    match = flat_slot[None, :] == order[:, None]
    pick = jnp.sum(match.astype(jnp.int32) * jnp.arange(width, dtype=jnp.int32)[None, :], axis=1)
    rows = received.reshape((width,) + received.shape[2:])
    owned = jnp.take(rows, pick, axis=0)
    count = jnp.take(received_count.reshape(-1), pick)
    context = shifted(last_two(owned, count), "tm", 1)
    first = first_section(owned, context, count, first_weight)
    half = (count + 1) // 2
    values = first.astype(jnp.float32)
    local_sum1 = jnp.sum(values, axis=(1, 2))
    local_sum2 = jnp.sum(values * values, axis=(1, 2))
    local_num = (half * places).astype(jnp.float32)
    zero_stats = jnp.zeros_like(local_sum1)
    prior = prefix(
        (local_sum1, local_sum2, local_num),
        "tm",
        add_stats,
        (zero_stats, zero_stats, jnp.zeros_like(local_num)),
    )
    sum1 = prior[0] + local_sum1
    sum2 = prior[1] + local_sum2
    num = prior[2] + local_num
    mean = sum1 / num[:, None]
    var = sum2 / num[:, None] - mean * mean
    normed = (values - mean[:, None, None, :]) * lax.rsqrt(var + 1e-05)[:, None, None, :] * gain
    normed = jnp.where(live_mask(count, first.shape[1], 2), normed, 0.0).astype(jnp.bfloat16)
    norm_ctx = shifted(last_two(normed, half), "tm", 1)
    second = causal_layer(normed, norm_ctx, second_weight) + bias
    encoded = jnp.where(live_mask(half, normed.shape[1] // 2, 2), second, 0.0).astype(jnp.bfloat16)
    return encoded[None]


def solution(mesh):
    return jax.shard_map(
        body,
        mesh=mesh,
        in_specs=(
            P("tm", "load", None, None, None),
            P("tm", "load"),
            P("load"),
            P(),
            P(),
            P(),
            P(),
        ),
        out_specs=P("tm", "load", None, None, None),
        check_vma=False,
    )
```

profile of v0, /device:TPU:448, one launch (start us, length us, event | category | flops | bytes accessed | tf_op | source)
XLA Modules:
  0.0 281.6 jit_solution(8483187637707688128)
XLA Ops:
  1.1 1.4 gather_fusion.6
  4.0 10.0 %all-to-all-start = ((s32[32,1,2]{2,1,0:T(1,128)}), s32[32,1,2]{2,1,0:T(1,128)S(1)}, u32[]{:S(2)}, u32[]{:S(2)}) async-start(s32[32,1,2]{2,1,0:T(1,128)} %bitcast.3), calls=%async_computation | async-start | bytes 32768 | tf_op jit(solution)/shard_map/all_to_all | solution.py:85
  14.9 2.1 bitcast_select_fusion
  18.0 3.6 %gather_fusion.1 = bf16[64,8,24,256]{3,2,1,0:T(8,128)(2,1)} fusion(bf16[32,8,24,256]{3,2,1,0:T(8,128)(2,1)S(1)} %bitcast_select_fusion, s32[1024]{0:T(1024)S(1)} %pad_clamp_fusion), kind=kCustom, calls=%fused_computation.3 | custom fusion | bytes 12583168 | tf_op jit(solution)/shard_map/jit(_take)/gather | solution.py:75
  21.6 2.1 all-to-all-done
  23.7 7.7 %all-to-all-start.1 = ((s32[32,1,2]{2,1,0:T(1,128)}), s32[32,1,2]{2,1,0:T(1,128)S(1)}, u32[]{:S(2)}, u32[]{:S(2)}) async-start(s32[32,1,2]{2,1,0:T(1,128)} %bitcast.5), calls=%async_computation.1 | async-start | bytes 32768 | tf_op jit(solution)/shard_map/all_to_all | solution.py:84
  31.4 6.2 %select_select_fusion = bf16[32,2,8,24,256]{4,3,2,1,0:T(8,128)(2,1)} fusion(bf16[32,2,8,24,256]{4,3,2,1,0:T(8,128)(2,1)} %bitcast.94, pred[32,2]{1,0:T(8,128)(4,1)S(1)} %copy.19, pred[32,2]{1,0:T(8,128)(4,1)S(1)} %broadcast_in_dim.159), kind=kLoop, calls=%fused_computation.12 | loop fusion | flops 6291456 | bytes 12583040 | tf_op jit(solution)/shard_map/jit(_where)/select_n | solution.py:76
  37.6 3.5 %all-to-all-done.1 = s32[32,1,2]{2,1,0:T(1,128)S(1)} async-done(((s32[32,1,2]{2,1,0:T(1,128)}), s32[32,1,2]{2,1,0:T(1,128)S(1)}, u32[]{:S(2)}, u32[]{:S(2)}) %all-to-all-start.1) | async-done | bytes 288 | tf_op jit(solution)/shard_map/all_to_all | solution.py:84
  41.1 6.4 %all-to-all-start.2 = ((bf16[32,2,8,24,256]{4,3,2,1,0:T(8,128)(2,1)}), bf16[32,2,8,24,256]{4,3,2,1,0:T(8,128)(2,1)}, u32[]{:S(2)}, u32[]{:S(2)}) async-start(bf16[32,2,8,24,256]{4,3,2,1,0:T(8,128)(2,1)} %select_select_fusion), calls=%async_computation.2 | async-start | bytes 12582912 | tf_op jit(solution)/shard_map/all_to_all | solution.py:77
  52.8 132.8 %all-to-all-done.2 = bf16[32,2,8,24,256]{4,3,2,1,0:T(8,128)(2,1)} async-done(((bf16[32,2,8,24,256]{4,3,2,1,0:T(8,128)(2,1)}), bf16[32,2,8,24,256]{4,3,2,1,0:T(8,128)(2,1)}, u32[]{:S(2)}, u32[]{:S(2)}) %all-to-all-start.2) | async-done | bytes 6291488 | tf_op jit(solution)/shard_map/all_to_all | solution.py:77
  185.6 5.2 %gather_fusion.2 = bf16[32,8,24,256]{3,2,1,0:T(8,128)(2,1)} fusion(bf16[64,8,24,256]{3,2,1,0:T(8,128)(2,1)} %bitcast.12, s32[1024]{0:T(1024)S(1)} %pad_clamp_fusion.1), kind=kCustom, calls=%fused_computation.4 | custom fusion | bytes 6291584 | tf_op jit(solution)/shard_map/jit(_take)/gather | solution.py:90
  190.8 2.2 broadcast_select_fusion
  193.1 1.6 gather_fusion.3
  194.7 1.3 broadcast_select_fusion.1
  195.9 1.9 collective-permute-start
  198.5 18.1 %all-gather.2 = f32[16,1,32]{2,1,0:T(1,128)} all-gather(f32[1,1,32]{2,1,0:T(1,128)S(1)} %convert_bitcast_fusion), channel_id=1, replica_groups=mesh['load'=32,'tm'=16] {'tm'}, dimensions={0}, use_global_device_ids=true | all-gather | bytes 2176 | tf_op jit(solution)/shard_map/all_gather | solution.py:17
  218.9 1.8 fusion.2
  220.8 16.8 %all-gather = f32[512,256]{1,0:T(8,128)S(1)} all-gather(f32[32,256]{1,0:T(8,128)S(1)} %get-tuple-element.55), channel_id=2, replica_groups=mesh['load'=32,'tm'=16] {'tm'}, dimensions={0}, use_global_device_ids=true | all-gather | bytes 557056 | tf_op jit(solution)/shard_map/all_gather | solution.py:17
  237.6 16.3 %all-gather.1 = f32[512,256]{1,0:T(8,128)S(1)} all-gather(f32[32,256]{1,0:T(8,128)S(1)} %get-tuple-element.54), channel_id=3, replica_groups=mesh['load'=32,'tm'=16] {'tm'}, dimensions={0}, use_global_device_ids=true | all-gather | bytes 557056 | tf_op jit(solution)/shard_map/all_gather | solution.py:17
  253.9 10.0 %while.14 = (s32[]{:T(128)}, f32[32,256]{1,0:T(8,128)S(1)}, f32[32,256]{1,0:T(8,128)S(1)}, f32[32]{0:T(128)S(1)}, s32[]{:T(128)}, /*index=5*/f32[16,32,256]{2,1,...) while((s32[]{:T(128)}, f32[32,256]{1,0:T(8,128)S(1)}, ...), condition=%wide.region_7.9_spmd, body=%wide.region_6.8_spmd.sunk | while | flops 16421 | bytes 197151 | solution.py:25
  264.1 1.4 fusion.6
  266.3 3.0 %collective-permute-start.1 = (bf16[32,2,24,256]{3,2,1,0:T(8,128)(2,1)S(1)}, bf16[32,2,24,256]{3,2,1,0:T(8,128)(2,1)S(1)}, u32[]{:S(2)}, u32[]{:S(2)}) collective-permute-start(bf16[32,2,24,256]{3,2,1,0:T(8,128)(2,1)S(1)} %broadcast_select_fusion.2), channel_id=1, source_target_pairs={{0,1},{1,2},{2,3},{3,4},{4,5},{5,6},{6,7},{7,8},{8,9},{9,10},{10,1... | collective-permute-start | bytes 2359304 | tf_op jit(solution)/shard_map/ppermute | solution.py:12
  269.8 9.8 %collective-permute-done.1 = bf16[32,2,24,256]{3,2,1,0:T(8,128)(2,1)S(1)} collective-permute-done((bf16[32,2,24,256]{3,2,1,0:T(8,128)(2,1)S(1)}, bf16[32,2,24,256]{3,2,1,0:T(8,128)(2,1)S(1)}, u32[]{:S(2)}, u32[]{:S(2)}) %collective-permute-start.1) | collective-permute-done | bytes 786464 | tf_op jit(solution)/shard_map/ppermute | solution.py:12
  280.2 1.4 fusion.12
  (101 shorter events, 24.5 us)
Async XLA Ops:
  4.0 19.7 %all-to-all-start = ((s32[32,1,2]{2,1,0:T(1,128)}), s32[32,1,2]{2,1,0:T(1,128)S(1)}, u32[]{:S(2)}, u32[]{:S(2)}) async-start(s32[32,1,2]{2,1,0:T(1,128)} %bitcast.3), calls=%async_computation | async-start | bytes 32768 | tf_op jit(solution)/shard_map/all_to_all | solution.py:85
  23.7 17.5 %all-to-all-start.1 = ((s32[32,1,2]{2,1,0:T(1,128)}), s32[32,1,2]{2,1,0:T(1,128)S(1)}, u32[]{:S(2)}, u32[]{:S(2)}) async-start(s32[32,1,2]{2,1,0:T(1,128)} %bitcast.5), calls=%async_computation.1 | async-start | bytes 32768 | tf_op jit(solution)/shard_map/all_to_all | solution.py:84
  41.1 144.5 %all-to-all-start.2 = ((bf16[32,2,8,24,256]{4,3,2,1,0:T(8,128)(2,1)}), bf16[32,2,8,24,256]{4,3,2,1,0:T(8,128)(2,1)}, u32[]{:S(2)}, u32[]{:S(2)}) async-start(bf16[32,2,8,24,256]{4,3,2,1,0:T(8,128)(2,1)} %select_select_fusion), calls=%async_computation.2 | async-start | bytes 12582912 | tf_op jit(solution)/shard_map/all_to_all | solution.py:77
  50.3 1.3 copy-start.7
  51.1 0.6 copy-start.5
  51.6 0.5 copy-start.4
  193.1 24.3 %copy-start.1 = (bf16[3,256,256]{2,1,0:T(8,128)(2,1)S(1)}, bf16[3,256,256]{2,1,0:T(8,128)(2,1)}, u32[]{:S(2)}) copy-start(bf16[3,256,256]{2,1,0:T(8,128)(2,1)} %param.14) | copy-start | bytes 1179652
  195.9 22.0 %collective-permute-start = (bf16[32,2,24,256]{3,2,1,0:T(8,128)(2,1)S(1)}, bf16[32,2,24,256]{3,2,1,0:T(8,128)(2,1)S(1)}, u32[]{:S(2)}, u32[]{:S(2)}) collective-permute-start(bf16[32,2,24,256]{3,2,1,0:T(8,128)(2,1)S(1)} %broadcast_select_fusion.1), channel_id=1, source_target_pairs={{0,1},{1,2},{2,3},{3,4},{4,5},{5,6},{6,7},{7,8},{8,9},{9,10},{10,1... | collective-permute-start | bytes 2359304 | tf_op jit(solution)/shard_map/ppermute | solution.py:12
  218.9 45.0 %copy-start.2 = (s32[32]{0:T(128)S(1)}, s32[32]{0:T(128)}, u32[]{:S(2)}) copy-start(s32[32]{0:T(128)} %get-tuple-element.73) | copy-start | bytes 388
  264.0 5.2 %copy-start.3 = (s32[32]{0:T(128)S(1)}, s32[32]{0:T(128)}, u32[]{:S(2)}) copy-start(s32[32]{0:T(128)} %get-tuple-element.73) | copy-start | bytes 388
  264.0 5.3 %copy-start = (bf16[3,256,256]{2,1,0:T(8,128)(2,1)S(1)}, bf16[3,256,256]{2,1,0:T(8,128)(2,1)}, u32[]{:S(2)}) copy-start(bf16[3,256,256]{2,1,0:T(8,128)(2,1)} %param.15) | copy-start | bytes 1179652
  266.3 13.3 %collective-permute-start.1 = (bf16[32,2,24,256]{3,2,1,0:T(8,128)(2,1)S(1)}, bf16[32,2,24,256]{3,2,1,0:T(8,128)(2,1)S(1)}, u32[]{:S(2)}, u32[]{:S(2)}) collective-permute-start(bf16[32,2,24,256]{3,2,1,0:T(8,128)(2,1)S(1)} %broadcast_select_fusion.2), channel_id=1, source_target_pairs={{0,1},{1,2},{2,3},{3,4},{4,5},{5,6},{6,7},{7,8},{8,9},{9,10},{10,1... | collective-permute-start | bytes 2359304 | tf_op jit(solution)/shard_map/ppermute | solution.py:12
  269.7 10.5 %copy-start.6 = (f32[256]{0:T(256)S(1)}, f32[256]{0:T(256)}, u32[]{:S(2)}) copy-start(f32[256]{0:T(256)} %param.17) | copy-start | bytes 3076
where the time goes:
time: 284 us; the launch traced here: 282 us
  waiting for transfers between devices  148 us (52%)
  blocking collectives  51.2 us (18%)
  other arithmetic  30.1 us (11%)
  starting transfers between devices  28.9 us (10%)
  local copies, waits for them, and re-layouts  17.5 us (6%)
  matrix products  5.18 us (2%)
    all_to_all x1, waiting for transfers between devices, body(): lax.all_to_all(taken.reshape((loads, CAP) + block.shape[1:]), 'load', spl...  133 us
    all_gather x3, blocking collectives, prefix(): gathered = jax.tree.map(lambda a: lax.all_gather(a, axis), part)  51.2 us
    all_to_all x1, starting transfers between devices, body(): lax.all_to_all(send_slot, 'load', split_axis=0, concat_axis=0, tiled=True)  9.95 us
    add x28, other arithmetic, add_stats(): return (earlier[0] + later[0], earlier[1] + later[1], earlier[2] + later[2])  9.95 us
    ppermute x2, waiting for transfers between devices, shifted(): lax.ppermute(value, axis, [(source, source + steps) for source in range(l...  9.83 us
    all_to_all x1, starting transfers between devices, body(): lax.all_to_all(send_count, 'load', split_axis=0, concat_axis=0, tiled=True)  7.68 us
    all_to_all x1, starting transfers between devices, body(): lax.all_to_all(taken.reshape((loads, CAP) + block.shape[1:]), 'load', spl...  6.36 us
    select_n x1, other arithmetic, body(): taken = jnp.where(filled[:, None, None, None], taken, jnp.zeros_like(taken))  6.24 us
  transfers between devices with their start and end apart: 5, of which 4 were waited for; matrix products, arithmetic and copies ran while one was open for 7% of the time, Pallas kernels for 0%

commit v1 on v0

v1 whole, which is shorter than its diff:
```python
import functools

import jax
import jax.numpy as jnp
from jax import lax
from jax.experimental import pallas as pl
from jax.experimental.pallas import tpu as pltpu
from jax.sharding import PartitionSpec as P

F32 = jnp.float32
BF16 = jnp.bfloat16
MESH = pl.DeviceIdType.MESH


def flat(x):
    videos, places, channels = x.shape
    return x.astype(F32).reshape(videos * places, channels).astype(BF16)


def dot(a, b):
    return jnp.dot(a, b, preferred_element_type=F32)


def silu(x):
    h = 0.5 * x
    return h + h * jnp.tanh(h)


def kernel(
    loads,
    spans,
    group,
    cnt_s,
    pack_s,
    cnt_v,
    dest_v,
    frames,
    w1,
    w2,
    gain,
    bias,
    out,
    tail,
    t1_send,
    t1_recv,
    t2_send,
    t2_recv,
    first,
    acc1,
    acc2,
    a_send,
    a_recv,
    b_send,
    b_recv,
    c_send,
    c_recv,
    mean_v,
    scale_v,
    enc_0,
    enc_1,
    stage,
    recv_0,
    recv_1,
    d_send,
    d_recv,
    table,
    sem_t,
    sem_b_send,
    sem_b_recv,
    sem_d_send,
    sem_d_recv,
    sem_x_send,
    sem_x_recv,
):
    videos, places, channels = frames.shape[0], frames.shape[2], frames.shape[3]
    length = frames.shape[1]
    chips = spans // 2
    half_c = channels // 2
    rows = group * places
    pairs = videos // 2
    me = lax.axis_index("load")
    t = lax.axis_index("tm")
    z = t // 2
    core = t % 2
    other = z * 2 + 1 - core
    after = lax.rem(t + 1, spans)
    beyond = lax.rem(t + jnp.where(core == 0, spans - 1, 1), spans)

    barrier = pltpu.get_barrier_semaphore()

    def greet(load, place):
        pl.semaphore_signal(barrier, inc=1, device_id=(load, place), device_id_type=MESH)

    greet(me, other)
    greet(me, beyond)

    @pl.loop(1, chips)
    def _(s):
        greet(me, lax.rem(z + s, chips) * 2 + core)

    @pl.loop(1, loads)
    def _(s):
        greet(lax.rem(me + s, loads), t)

    @pl.loop(0, videos)
    def _(v):
        tail[0, v] = frames[v, jnp.clip(cnt_s[0, v] - 2, 0, length - 1)]
        tail[1, v] = frames[v, jnp.clip(cnt_s[0, v] - 1, 0, length - 1)]

    @pl.loop(0, videos // group)
    def _(g):
        at = pl.ds(g * group, group)
        lhs = jnp.concatenate([flat(tail[0, at]), flat(tail[1, at])], axis=1)
        t1_send[pl.ds(pl.multiple_of(g * rows, rows), rows)] = dot(lhs, w1[: 2 * channels]).astype(BF16)

    lanes = 128
    row = jnp.pad(dest_v[...], ((0, 7), (0, lanes - videos)), constant_values=-1)
    d_send[...] = row

    pl.semaphore_wait(barrier, 1 + 1 + (chips - 1) + (loads - 1))

    def remote(src, dst, ss, rs, load, place):
        return pltpu.make_async_remote_copy(
            src_ref=src, dst_ref=dst, send_sem=ss, recv_sem=rs, device_id=(load, place), device_id_type=MESH
        )

    t1 = remote(t1_send, t1_recv, sem_t.at[0], sem_t.at[1], me, after)
    t1.start()

    @pl.loop(1, loads)
    def _(s):
        remote(d_send, d_recv.at[me], sem_d_send.at[s], sem_d_recv.at[s], lax.rem(me + s, loads), t).start()

    d_recv[me] = row

    def column(values):
        r = lax.broadcasted_iota(jnp.int32, (videos, videos), 0)
        c = lax.broadcasted_iota(jnp.int32, (videos, videos), 1)
        return jnp.sum(jnp.where(r == c, values, 0), axis=1, keepdims=True)

    counts_row = cnt_v[...]

    def add_sums(g, at, values, fresh):
        tiles = values.reshape(group, places // 8, 8, channels)
        s1 = jnp.sum(tiles, axis=1)
        s2 = jnp.sum(tiles * tiles, axis=1)
        if fresh:
            acc1[at] = s1
            acc2[at] = s2
        else:
            acc1[at] += s1
            acc2[at] += s2

    def group_live(g, step, limit_of):
        parts = [limit_of(cnt_s[0, g * group + i]) > step for i in range(group)]
        return parts

    def masked(value, flags):
        pieces = value.reshape(group, places, channels)
        return jnp.concatenate(
            [jnp.where(flags[i], pieces[i : i + 1], 0.0) for i in range(group)], axis=0
        )

    @pl.loop(0, videos // group)
    def _(g):
        at = pl.ds(g * group, group)
        place = pl.ds(pl.multiple_of(g * rows, rows), rows)
        for j in range(1, 4):
            lhs = jnp.concatenate([flat(frames[at, 2 * j - 2 + k]) for k in range(3)], axis=1)
            value = masked(silu(dot(lhs, w1[...])), group_live(g, 2 * j, lambda n: n))
            value = value.reshape(rows, channels).astype(BF16)
            first[j, place] = value
            add_sums(g, at, value.astype(F32), j == 1)

    t1.wait_recv()

    @pl.loop(0, videos // group)
    def _(g):
        at = pl.ds(g * group, group)
        place = pl.ds(pl.multiple_of(g * rows, rows), rows)
        part = jnp.where(t > 0, t1_recv[place].astype(F32), 0.0)
        value = silu(part + dot(flat(frames[at, 0]), w1[2 * channels :])).astype(BF16)
        first[0, place] = value
        add_sums(g, at, value.astype(F32), False)

    s1 = jnp.sum(acc1[...], axis=1)
    s2 = jnp.sum(acc2[...], axis=1)
    num = (((counts_row + 1) // 2) * places).astype(F32)
    num = jnp.pad(num, ((0, 7), (0, lanes - videos)))
    low = core == 0
    enc = (enc_0, enc_1)
    recv = (recv_0, recv_1)

    def mine(x):
        return jnp.where(low, x[:, :half_c], x[:, half_c:])

    def others(x):
        return jnp.where(low, x[:, half_c:], x[:, :half_c])

    a_send[...] = jnp.concatenate([others(s1), others(s2), num], axis=0)
    a_copy = remote(a_send, a_recv, sem_t.at[2], sem_t.at[3], me, other)
    a_copy.start()
    own = jnp.concatenate([mine(s1), mine(s2), num], axis=0)
    a_copy.wait_recv()
    theirs = a_recv[...]
    chip = own + theirs
    b_send[...] = chip

    @pl.loop(1, chips)
    def _(s):
        remote(
            b_send, b_recv.at[s - 1], sem_b_send.at[s - 1], sem_b_recv.at[s - 1], me, lax.rem(z + s, chips) * 2 + core
        ).start()

    even = jnp.where(low, own, theirs)
    base = jnp.zeros_like(own)
    for s in range(1, chips):
        remote(b_send, b_recv.at[s - 1], sem_b_send.at[s - 1], sem_b_recv.at[s - 1], me, other).wait_recv()
        base = base + jnp.where(z >= s, b_recv[s - 1], 0.0)

    my_gain = mine(gain[...])

    def finish(total):
        count = column(total[2 * videos : 2 * videos + 1, :videos])
        mean = total[:videos] / count
        var = total[videos : 2 * videos] / count - mean * mean
        return jnp.concatenate([mean, lax.rsqrt(var + 1e-05) * my_gain], axis=0)

    on_even = finish(base + even)
    on_odd = finish(base + chip)
    c_send[...] = jnp.where(low, on_odd, on_even)
    c_copy = remote(c_send, c_recv, sem_t.at[4], sem_t.at[5], me, other)
    c_copy.start()
    here = jnp.where(low, on_even, on_odd)
    c_copy.wait_recv()
    there = c_recv[...]
    both = jnp.concatenate([jnp.where(low, here, there), jnp.where(low, there, here)], axis=1)
    mean_v[...] = both[:videos]
    scale_v[...] = both[videos:]

    @pl.loop(0, videos // group)
    def _(g):
        at = pl.ds(pl.multiple_of(g * group, group), group)
        place = pl.ds(pl.multiple_of(g * rows, rows), rows)
        mean = mean_v[at][:, None, :]
        scale = scale_v[at][:, None, :]
        normed = []
        for j in range(4):
            value = first[j, place].astype(F32).reshape(group, places, channels)
            value = (value - mean) * scale
            normed.append(value)
            first[j, place] = value.reshape(rows, channels).astype(BF16)
        ends = []
        for k in range(2):
            pieces = []
            for i in range(group):
                n = (cnt_s[0, g * group + i] + 1) // 2
                pieces.append(
                    jnp.where(
                        n == 2,
                        normed[k][i : i + 1],
                        jnp.where(n == 3, normed[k + 1][i : i + 1], normed[k + 2][i : i + 1]),
                    )
                )
            ends.append(jnp.concatenate(pieces, axis=0).reshape(rows, channels).astype(BF16))
        t2_send[place] = dot(jnp.concatenate(ends, axis=1), w2[: 2 * channels]).astype(BF16)

    t2 = remote(t2_send, t2_recv, sem_t.at[6], sem_t.at[7], me, after)
    t2.start()

    def exchange(i):
        stage[i, me, 0] = enc[i][pack_s[2 * me]]
        stage[i, me, 1] = enc[i][pack_s[2 * me + 1]]
        recv[i][me] = stage[i, me]

        @pl.loop(1, loads)
        def _(s):
            to = lax.rem(me + s, loads)
            stage[i, to, 0] = enc[i][pack_s[2 * to]]
            stage[i, to, 1] = enc[i][pack_s[2 * to + 1]]
            remote(stage.at[i, to], recv[i].at[me], sem_x_send.at[i, s], sem_x_recv.at[i, s], to, t).start()

    @pl.loop(0, videos // group)
    def _(g):
        at = pl.ds(g * group, group)
        place = pl.ds(pl.multiple_of(g * rows, rows), rows)
        lhs = jnp.concatenate([first[j, place] for j in range(3)], axis=1)
        value = masked(dot(lhs, w2[...]) + bias[...], group_live(g, 2, lambda n: (n + 1) // 2))
        enc_1[at] = value.astype(BF16)

    exchange(1)
    t2.wait_recv()

    @pl.loop(0, videos // group)
    def _(g):
        at = pl.ds(g * group, group)
        place = pl.ds(pl.multiple_of(g * rows, rows), rows)
        part = jnp.where(t > 0, t2_recv[place].astype(F32), 0.0)
        value = part + dot(first[0, place], w2[2 * channels :]) + bias[...]
        enc_0[at] = value.reshape(group, places, channels).astype(BF16)

    exchange(0)

    @pl.loop(1, loads)
    def _(s):
        remote(
            d_send, d_recv.at[lax.rem(me + loads - s, loads)], sem_d_send.at[s], sem_d_recv.at[s], me, other
        ).wait_recv()

    known = d_recv[...][:, 0, :]
    loader = lax.broadcasted_iota(jnp.int32, known.shape, 0)
    for i in range(pairs):
        table[i] = jnp.clip(jnp.sum(jnp.where(known == me * videos + 2 * i, loader, 0)), 0, loads - 1)

    for i in (1, 0):

        @pl.loop(1, loads)
        def _(s):
            remote(
                stage.at[i, 0],
                recv[i].at[lax.rem(me + loads - s, loads)],
                sem_x_send.at[i, s],
                sem_x_recv.at[i, s],
                me,
                other,
            ).wait_recv()

        @pl.loop(0, pairs)
        def _(q):
            out[2 * q, i] = recv[i][table[q], 0]
            out[2 * q + 1, i] = recv[i][table[q], 1]

    t1.wait_send()
    t2.wait_send()
    a_copy.wait_send()
    c_copy.wait_send()

    @pl.loop(1, chips)
    def _(s):
        remote(b_send, b_recv.at[s - 1], sem_b_send.at[s - 1], sem_b_recv.at[s - 1], me, other).wait_send()

    @pl.loop(1, loads)
    def _(s):
        remote(d_send, d_recv.at[me], sem_d_send.at[s], sem_d_recv.at[s], me, other).wait_send()
        for i in range(2):
            remote(stage.at[i, 0], recv[i].at[me], sem_x_send.at[i, s], sem_x_recv.at[i, s], me, other).wait_send()


def body(loads, spans, frames, counts, dest, first_weight, second_weight, gain, bias):
    videos, length, places, channels = frames.shape[1:]
    group = min(8, videos)
    rows = videos * places
    chips = spans // 2
    slot = dest // videos * 2 + dest % 2
    hit = slot[None, :] == jnp.arange(2 * loads, dtype=jnp.int32)[:, None]
    pack = jnp.sum(jnp.where(hit, jnp.arange(videos, dtype=jnp.int32)[None, :], 0), axis=1)
    vmem = pl.BlockSpec(memory_space=pltpu.VMEM)
    smem = pl.BlockSpec(memory_space=pltpu.SMEM)
    message = (2 * videos + 8, 128)
    result = pl.pallas_call(
        functools.partial(kernel, loads, spans, group),
        out_shape=jax.ShapeDtypeStruct((videos, 2, places, channels), BF16),
        in_specs=[smem, smem] + [vmem] * 7,
        out_specs=vmem,
        scratch_shapes=[
            pltpu.VMEM((2, videos, places, channels), BF16),
            pltpu.VMEM((rows, channels), BF16),
            pltpu.VMEM((rows, channels), BF16),
            pltpu.VMEM((rows, channels), BF16),
            pltpu.VMEM((rows, channels), BF16),
            pltpu.VMEM((4, rows, channels), BF16),
            pltpu.VMEM((videos, 8, channels), F32),
            pltpu.VMEM((videos, 8, channels), F32),
            pltpu.VMEM(message, F32),
            pltpu.VMEM(message, F32),
            pltpu.VMEM(message, F32),
            pltpu.VMEM((chips - 1,) + message, F32),
            pltpu.VMEM((2 * videos, 128), F32),
            pltpu.VMEM((2 * videos, 128), F32),
            pltpu.VMEM((videos, channels), F32),
            pltpu.VMEM((videos, channels), F32),
            pltpu.VMEM((videos, places, channels), BF16),
            pltpu.VMEM((videos, places, channels), BF16),
            pltpu.VMEM((2, loads, 2, places, channels), BF16),
            pltpu.VMEM((loads, 2, places, channels), BF16),
            pltpu.VMEM((loads, 2, places, channels), BF16),
            pltpu.VMEM((8, 128), jnp.int32),
            pltpu.VMEM((loads, 8, 128), jnp.int32),
            pltpu.SMEM((videos // 2,), jnp.int32),
            pltpu.SemaphoreType.DMA((8,)),
            pltpu.SemaphoreType.DMA((chips - 1,)),
            pltpu.SemaphoreType.DMA((chips - 1,)),
            pltpu.SemaphoreType.DMA((loads,)),
            pltpu.SemaphoreType.DMA((loads,)),
            pltpu.SemaphoreType.DMA((2, loads)),
            pltpu.SemaphoreType.DMA((2, loads)),
        ],
        compiler_params=pltpu.CompilerParams(
            collective_id=0, has_side_effects=True, vmem_limit_bytes=48 * 1024 * 1024
        ),
    )(
        counts,
        pack,
        counts,
        dest.reshape(1, videos),
        frames[0],
        first_weight.reshape(3 * channels, channels),
        second_weight.reshape(3 * channels, channels),
        gain.reshape(1, channels),
        bias.reshape(1, channels),
    )
    return result[None]


def solution(mesh):
    loads, spans = mesh.shape["load"], mesh.shape["tm"]
    return jax.shard_map(
        functools.partial(body, loads, spans),
        mesh=mesh,
        in_specs=(
            P("tm", "load", None, None, None),
            P("tm", "load"),
            P("load"),
            P(),
            P(),
            P(),
            P(),
        ),
        out_specs=P("tm", "load", None, None, None),
        check_vma=False,
    )
```

time: 284 us -> 84.2 us (0.30)
  the two profiles are of different devices: /device:TPU:448 before, /device:TPU:4 now
where the time goes in v1:
time: 84.2 us; the launch traced here: 83.9 us
  Pallas kernels  75.7 us (90%)
  local copies, waits for them, and re-layouts  7.43 us (9%)
    pallas_call x1, Pallas kernels, body(): pl.pallas_call(functools.partial(kernel, loads, spans, group), out_shape=...  75.7 us
    unnamed x15, local copies, waits for them, and re-layouts  7.43 us

profile of v1, /device:TPU:4, one launch (start us, length us, event | category | flops | bytes accessed | tf_op | source)
XLA Modules:
  0.0 83.9 jit_solution(17433212759068252825)
XLA Ops:
  0.0 0.7 fusion
  0.7 0.1 select_reduce_fusion.pack_s
  0.8 0.0 copy-start
  0.8 1.9 %copy-done = bf16[1,32,8,24,256]{4,3,2,1,0:T(8,128)(2,1)S(1)} copy-done((bf16[1,32,8,24,256]{4,3,2,1,0:T(8,128)(2,1)S(1)}, bf16[1,32,8,24,256]{4,3,2,1,0:T(8,128)(2,1)}, u32[]{:S(2)}) %copy-start) | copy-done | bytes 3145752
  2.6 0.0 copy-start.1
  2.7 1.0 %copy-done.1 = bf16[3,256,256]{2,1,0:T(8,128)(2,1)S(1)} copy-done((bf16[3,256,256]{2,1,0:T(8,128)(2,1)S(1)}, bf16[3,256,256]{2,1,0:T(8,128)(2,1)}, u32[]{:S(2)}) %copy-start.1) | copy-done | bytes 393240
  3.6 0.0 copy-start.2
  3.6 1.0 %copy-done.2 = bf16[3,256,256]{2,1,0:T(8,128)(2,1)S(1)} copy-done((bf16[3,256,256]{2,1,0:T(8,128)(2,1)S(1)}, bf16[3,256,256]{2,1,0:T(8,128)(2,1)}, u32[]{:S(2)}) %copy-start.2) | copy-done | bytes 393240
  4.6 0.0 copy-start.3
  4.6 0.7 copy-done.3
  5.3 0.0 copy-start.4
  5.3 0.7 copy-done.4
  6.0 0.0 copy-start.5
  6.0 0.7 copy-done.5
  6.7 0.0 copy-start.6
  6.7 0.7 copy-done.6
  7.3 75.7 %shard_map.73 = bf16[32,2,24,256]{3,2,1,0:T(8,128)(2,1)S(1)} custom-call(s32[1,32]{1,0:T(1,128)S(1)} %copy-done.3, s32[64]{0:T(128)S(1)} %select_reduce_fusion.pack_s, s32[1,32]{1,0:T(1,128)S(1)} %copy-done.3, s32[1,32]{1,0:T(1,128)S(1)} %bitcast.13, bf16[32,8,24,256]{3,2,1,0:T(8,128)(2,1)S(1)} %bitcast.7, bf16[768,256]{1,0:T(8,128)(2,1)S(1)} %bitcast.9, ...), custom_call_target="tpu_custom_call" | custom-call | tf_op jit(solution)/shard_map/pallas_call | solution.py:360
  83.0 0.9 %copy.9 = bf16[1,32,2,24,256]{4,3,2,1,0:T(8,128)(2,1)} copy(bf16[1,32,2,24,256]{4,3,2,1,0:T(8,128)(2,1)S(1)} %bitcast.8) | data formatting | bytes 1572864
Async XLA Ops:
  0.8 1.9 %copy-start = (bf16[1,32,8,24,256]{4,3,2,1,0:T(8,128)(2,1)S(1)}, bf16[1,32,8,24,256]{4,3,2,1,0:T(8,128)(2,1)}, u32[]{:S(2)}) copy-start(bf16[1,32,8,24,256]{4,3,2,1,0:T(8,128)(2,1)} %param.7) | copy-start | bytes 9437188
  2.6 1.0 %copy-start.1 = (bf16[3,256,256]{2,1,0:T(8,128)(2,1)S(1)}, bf16[3,256,256]{2,1,0:T(8,128)(2,1)}, u32[]{:S(2)}) copy-start(bf16[3,256,256]{2,1,0:T(8,128)(2,1)} %param.10) | copy-start | bytes 1179652
  3.6 1.0 %copy-start.2 = (bf16[3,256,256]{2,1,0:T(8,128)(2,1)S(1)}, bf16[3,256,256]{2,1,0:T(8,128)(2,1)}, u32[]{:S(2)}) copy-start(bf16[3,256,256]{2,1,0:T(8,128)(2,1)} %param.11) | copy-start | bytes 1179652
  4.6 0.7 copy-start.3
  5.3 0.7 copy-start.4
  6.0 0.7 copy-start.5
  6.7 0.7 copy-start.6

commit v2 on v1

v2 whole, which is shorter than its diff:
```python
import functools

import jax
import jax.numpy as jnp
from jax import lax
from jax.experimental import pallas as pl
from jax.experimental.pallas import tpu as pltpu
from jax.sharding import PartitionSpec as P

F32 = jnp.float32
BF16 = jnp.bfloat16
MESH = pl.DeviceIdType.MESH


def flat(x):
    videos, places, channels = x.shape
    return x.astype(F32).reshape(videos * places, channels).astype(BF16)


def dot(a, b):
    return jnp.dot(a, b, preferred_element_type=F32)


def silu(x):
    h = 0.5 * x
    return h + h * jnp.tanh(h)


def kernel(
    loads,
    spans,
    group,
    counts_hbm,
    dest_hbm,
    frames_hbm,
    w1_hbm,
    w2_hbm,
    gain_hbm,
    bias_hbm,
    out,
    cnt_s,
    cnt_v,
    dest_v,
    frames,
    w1,
    w2,
    gain,
    bias,
    pack_v,
    pack_s,
    tail,
    t1_send,
    t1_recv,
    t2_send,
    t2_recv,
    first,
    acc1,
    acc2,
    a_send,
    a_recv,
    b_send,
    b_recv,
    c_send,
    c_recv,
    mean_v,
    scale_v,
    enc_0,
    enc_1,
    stage,
    recv_0,
    recv_1,
    d_send,
    d_recv,
    table,
    sem_in,
    sem_t,
    sem_c_send,
    sem_c_recv,
    sem_a_send,
    sem_a_recv,
    sem_b_send,
    sem_b_recv,
    sem_s_send,
    sem_s_recv,
    sem_x_send,
    sem_x_recv,
):
    videos, places, channels = frames.shape[0], frames.shape[2], frames.shape[3]
    length = frames.shape[1]
    teams = spans // 4
    quarter = channels // 4
    rows = group * places
    pairs = videos // 2
    me = lax.axis_index("load")
    t = lax.axis_index("tm")
    team = t // 4
    seat = t % 4
    after = lax.rem(t + 1, spans)
    beyond = lax.rem(t + jnp.where(seat == 0, spans - 1, 1), spans)
    edge = jnp.logical_or(seat == 0, seat == 3)

    pieces = 4
    part = videos // pieces
    fetches = [
        pltpu.make_async_copy(a, b, sem_in.at[i])
        for i, (a, b) in enumerate(
            [(counts_hbm, cnt_s), (counts_hbm, cnt_v), (dest_hbm, dest_v)]
            + [(frames_hbm.at[pl.ds(q * part, part)], frames.at[pl.ds(q * part, part)]) for q in range(pieces)]
            + [(w1_hbm, w1), (w2_hbm, w2), (gain_hbm, gain), (bias_hbm, bias)]
        )
    ]
    for fetch in fetches:
        fetch.start()

    enc = (enc_0, enc_1)
    recv = (recv_0, recv_1)
    barrier = pltpu.get_barrier_semaphore()

    def greet(load, place):
        pl.semaphore_signal(barrier, inc=1, device_id=(load, place), device_id_type=MESH)

    @pl.when(edge)
    def _():
        greet(me, beyond)

    for s in range(1, 4):
        greet(me, team * 4 + lax.rem(seat + s, 4))
    for s in range(1, teams):
        greet(me, lax.rem(team + s, teams) * 4 + seat)

    @pl.loop(1, loads)
    def _(s):
        greet(lax.rem(me + s, loads), t)

    for fetch in fetches[:-3]:
        fetch.wait()

    @pl.loop(0, videos)
    def _(v):
        tail[0, v] = frames[v, jnp.clip(cnt_s[0, v] - 2, 0, length - 1)]
        tail[1, v] = frames[v, jnp.clip(cnt_s[0, v] - 1, 0, length - 1)]

    @pl.loop(0, videos // group)
    def _(g):
        at = pl.ds(g * group, group)
        lhs = jnp.concatenate([flat(tail[0, at]), flat(tail[1, at])], axis=1)
        t1_send[pl.ds(pl.multiple_of(g * rows, rows), rows)] = dot(lhs, w1[: 2 * channels]).astype(BF16)

    lanes = 128
    row = jnp.pad(dest_v[...], ((0, 7), (0, lanes - videos)), constant_values=-1)
    d_send[...] = row

    pl.semaphore_wait(barrier, 3 + (teams - 1) + (loads - 1) + jnp.where(edge, 1, 0))

    def remote(src, dst, ss, rs, load, place):
        return pltpu.make_async_remote_copy(
            src_ref=src, dst_ref=dst, send_sem=ss, recv_sem=rs, device_id=(load, place), device_id_type=MESH
        )

    def context(g):
        place = pl.ds(pl.multiple_of(g * rows, rows), rows)
        return remote(t1_send.at[place], t1_recv.at[place], sem_c_send.at[g], sem_c_recv.at[g], me, after)

    for g in range(videos // group):
        context(g).start()

    d_recv[me] = row

    def column(values):
        r = lax.broadcasted_iota(jnp.int32, (videos, videos), 0)
        c = lax.broadcasted_iota(jnp.int32, (videos, videos), 1)
        return jnp.sum(jnp.where(r == c, values, 0), axis=1, keepdims=True)

    for fetch in fetches[-3:]:
        fetch.wait()
    counts_row = cnt_v[...]

    place_of = column(dest_v[...])
    place_of = place_of // videos * 2 + place_of % 2
    lane = lax.broadcasted_iota(jnp.int32, (videos, 128), 1)
    video = lax.broadcasted_iota(jnp.int32, (videos, 128), 0)
    pack_v[...] = jnp.clip(jnp.sum(jnp.where(place_of == lane, video, 0), axis=0, keepdims=True), 0, videos - 1)
    to_scalars = pltpu.make_async_copy(pack_v, pack_s, sem_in.at[len(fetches)])
    to_scalars.start()

    def add_sums(g, at, values, fresh):
        tiles = values.reshape(group, places // 8, 8, channels)
        s1 = jnp.sum(tiles, axis=1)
        s2 = jnp.sum(tiles * tiles, axis=1)
        if fresh:
            acc1[at] = s1
            acc2[at] = s2
        else:
            acc1[at] += s1
            acc2[at] += s2

    def group_live(g, step, limit_of):
        parts = [limit_of(cnt_s[0, g * group + i]) > step for i in range(group)]
        return parts

    def masked(value, flags):
        pieces = value.reshape(group, places, channels)
        return jnp.concatenate(
            [jnp.where(flags[i], pieces[i : i + 1], 0.0) for i in range(group)], axis=0
        )

    @pl.loop(0, videos // group)
    def _(g):
        at = pl.ds(g * group, group)
        place = pl.ds(pl.multiple_of(g * rows, rows), rows)
        for j in range(1, 4):
            lhs = jnp.concatenate([flat(frames[at, 2 * j - 2 + k]) for k in range(3)], axis=1)
            value = masked(silu(dot(lhs, w1[...])), group_live(g, 2 * j, lambda n: n))
            value = value.reshape(rows, channels).astype(BF16)
            first[j, place] = value
            add_sums(g, at, value.astype(F32), j == 1)

    @pl.loop(1, loads)
    def _(s):
        remote(d_send, d_recv.at[me], sem_t.at[2], sem_t.at[3], lax.rem(me + s, loads), t).start()

    to_scalars.wait()

    @pl.loop(0, videos // group)
    def _(g):
        at = pl.ds(g * group, group)
        place = pl.ds(pl.multiple_of(g * rows, rows), rows)
        context(g).wait_recv()
        part = jnp.where(t > 0, t1_recv[place].astype(F32), 0.0)
        value = silu(part + dot(flat(frames[at, 0]), w1[2 * channels :])).astype(BF16)
        first[0, place] = value
        add_sums(g, at, value.astype(F32), False)

    s1 = jnp.sum(acc1[...], axis=1)
    s2 = jnp.sum(acc2[...], axis=1)
    num = (((counts_row + 1) // 2) * places).astype(F32)
    num = jnp.pad(num, ((0, 7), (0, lanes - videos)))

    def parts(x):
        return [x[:, r * quarter : (r + 1) * quarter] for r in range(4)]

    for r, (p1, p2) in enumerate(zip(parts(s1), parts(s2))):
        a_send[r] = jnp.concatenate([jnp.concatenate([p1, p2], axis=1), num], axis=0)

    def mates(source, target, ss, rs):
        made = []
        for s in range(1, 4):
            mate = lax.rem(seat + s, 4)
            made.append(
                remote(source.at[mate], target.at[seat], ss.at[s - 1], rs.at[s - 1], me, team * 4 + mate)
            )
        return made

    a_copies = mates(a_send, a_recv, sem_a_send, sem_a_recv)
    for copy in a_copies:
        copy.start()
    a_recv[seat] = a_send[seat]
    my_gain = sum(jnp.where(seat == r, g, 0.0) for r, g in enumerate(parts(gain[...])))
    my_gain = jnp.concatenate([my_gain, my_gain], axis=1)
    for s in range(1, 4):
        from_mate = lax.rem(seat + 4 - s, 4)
        remote(
            a_send.at[0], a_recv.at[from_mate], sem_a_send.at[s - 1], sem_a_recv.at[s - 1], me, after
        ).wait_recv()
    totals = [a_recv[0]]
    for r in range(1, 4):
        totals.append(totals[-1] + a_recv[r])
    b_send[...] = totals[-1]
    b_copies = [
        remote(
            b_send,
            b_recv.at[s - 1],
            sem_b_send.at[s - 1],
            sem_b_recv.at[s - 1],
            me,
            lax.rem(team + s, teams) * 4 + seat,
        )
        for s in range(1, teams)
    ]
    for copy in b_copies:
        copy.start()
    base = jnp.zeros_like(totals[0])
    for s, copy in enumerate(b_copies, 1):
        copy.wait_recv()
        base = base + jnp.where(team >= s, b_recv[s - 1], 0.0)

    in_low = lax.broadcasted_iota(jnp.int32, (videos, lanes), 1) < quarter
    for r in range(4):
        total = base + totals[r]
        value = total[:videos] / column(total[videos : videos + 1, :videos])
        swapped = jnp.concatenate([value[:, quarter:], value[:, :quarter]], axis=1)
        var = value - swapped * swapped
        c_send[r] = jnp.where(in_low, value, lax.rsqrt(var + 1e-05) * my_gain)
    c_copies = mates(c_send, c_recv, sem_s_send, sem_s_recv)
    for copy in c_copies:
        copy.start()
    c_recv[seat] = c_send[seat]
    for s in range(1, 4):
        from_mate = lax.rem(seat + 4 - s, 4)
        remote(
            c_send.at[0], c_recv.at[from_mate], sem_s_send.at[s - 1], sem_s_recv.at[s - 1], me, after
        ).wait_recv()
    mean_v[...] = jnp.concatenate([c_recv[r][:, :quarter] for r in range(4)], axis=1)
    scale_v[...] = jnp.concatenate([c_recv[r][:, quarter:] for r in range(4)], axis=1)

    def exchange(i):
        stage[i, me, 0] = enc[i][pack_s[0, 2 * me]]
        stage[i, me, 1] = enc[i][pack_s[0, 2 * me + 1]]
        recv[i][me] = stage[i, me]

        @pl.loop(1, loads)
        def _(s):
            to = lax.rem(me + s, loads)
            stage[i, to, 0] = enc[i][pack_s[0, 2 * to]]
            stage[i, to, 1] = enc[i][pack_s[0, 2 * to + 1]]
            remote(stage.at[i, to], recv[i].at[me], sem_x_send.at[i], sem_x_recv.at[i], to, t).start()

    def all_of(i):
        sent = pl.ds(0, loads - 1)
        return remote(stage.at[i, sent], recv[i].at[sent], sem_x_send.at[i], sem_x_recv.at[i], me, after)

    @pl.loop(0, videos // group)
    def _(g):
        at = pl.ds(pl.multiple_of(g * group, group), group)
        place = pl.ds(pl.multiple_of(g * rows, rows), rows)
        mean = mean_v[at][:, None, :]
        scale = scale_v[at][:, None, :]
        taps = []
        for j in range(4):
            value = first[j, place].astype(F32).reshape(group, places, channels)
            value = ((value - mean) * scale).reshape(rows, channels).astype(BF16)
            first[j, place] = value
            taps.append(value)
        lhs = jnp.concatenate(taps[:3], axis=1)
        value = masked(dot(lhs, w2[...]) + bias[...], group_live(g, 2, lambda n: (n + 1) // 2))
        enc_1[at] = value.astype(BF16)

    exchange(1)

    @pl.loop(0, videos // group)
    def _(g):
        place = pl.ds(pl.multiple_of(g * rows, rows), rows)
        normed = [first[j, place].astype(F32).reshape(group, places, channels) for j in range(4)]
        ends = []
        for k in range(2):
            pieces = []
            for i in range(group):
                n = (cnt_s[0, g * group + i] + 1) // 2
                pieces.append(
                    jnp.where(
                        n == 2,
                        normed[k][i : i + 1],
                        jnp.where(n == 3, normed[k + 1][i : i + 1], normed[k + 2][i : i + 1]),
                    )
                )
            ends.append(jnp.concatenate(pieces, axis=0).reshape(rows, channels).astype(BF16))
        t2_send[place] = dot(jnp.concatenate(ends, axis=1), w2[: 2 * channels]).astype(BF16)

    t2 = remote(t2_send, t2_recv, sem_t.at[0], sem_t.at[1], me, after)
    t2.start()
    t2.wait_recv()

    @pl.loop(0, videos // group)
    def _(g):
        at = pl.ds(g * group, group)
        place = pl.ds(pl.multiple_of(g * rows, rows), rows)
        part = jnp.where(t > 0, t2_recv[place].astype(F32), 0.0)
        value = part + dot(first[0, place], w2[2 * channels :]) + bias[...]
        enc_0[at] = value.reshape(group, places, channels).astype(BF16)

    exchange(0)

    others = pl.ds(0, loads - 1)
    remote(d_recv.at[others], d_recv.at[others], sem_t.at[2], sem_t.at[3], me, after).wait()
    known = d_recv[...][:, 0, :]
    loader = lax.broadcasted_iota(jnp.int32, known.shape, 0)
    for i in range(pairs):
        table[i] = jnp.clip(jnp.sum(jnp.where(known == me * videos + 2 * i, loader, 0)), 0, loads - 1)

    for g in range(videos // group):
        context(g).wait_send()
    for copy in [t2] + a_copies + b_copies + c_copies:
        copy.wait_send()

    for i in (1, 0):
        all_of(i).wait_recv()

        @pl.loop(0, pairs)
        def _(q):
            out[2 * q, i] = recv[i][table[q], 0]
            out[2 * q + 1, i] = recv[i][table[q], 1]

        all_of(i).wait_send()


def body(loads, spans, frames, counts, dest, first_weight, second_weight, gain, bias):
    videos, length, places, channels = frames.shape[1:]
    group = min(16, videos)
    rows = videos * places
    vmem = pl.BlockSpec(memory_space=pltpu.VMEM)
    hbm = pl.BlockSpec(memory_space=pltpu.HBM)
    message = (videos + 8, 128)
    result = pl.pallas_call(
        functools.partial(kernel, loads, spans, group),
        out_shape=jax.ShapeDtypeStruct((videos, 2, places, channels), BF16),
        in_specs=[hbm] * 7,
        out_specs=vmem,
        scratch_shapes=[
            pltpu.SMEM((1, videos), jnp.int32),
            pltpu.VMEM((1, videos), jnp.int32),
            pltpu.VMEM((1, videos), jnp.int32),
            pltpu.VMEM((videos, length, places, channels), BF16),
            pltpu.VMEM((3 * channels, channels), BF16),
            pltpu.VMEM((3 * channels, channels), BF16),
            pltpu.VMEM((1, channels), F32),
            pltpu.VMEM((1, channels), F32),
            pltpu.VMEM((1, 128), jnp.int32),
            pltpu.SMEM((1, 128), jnp.int32),
            pltpu.VMEM((2, videos, places, channels), BF16),
            pltpu.VMEM((rows, channels), BF16),
            pltpu.VMEM((rows, channels), BF16),
            pltpu.VMEM((rows, channels), BF16),
            pltpu.VMEM((rows, channels), BF16),
            pltpu.VMEM((4, rows, channels), BF16),
            pltpu.VMEM((videos, 8, channels), F32),
            pltpu.VMEM((videos, 8, channels), F32),
            pltpu.VMEM((4,) + message, F32),
            pltpu.VMEM((4,) + message, F32),
            pltpu.VMEM(message, F32),
            pltpu.VMEM((spans // 4 - 1,) + message, F32),
            pltpu.VMEM((4, videos, 128), F32),
            pltpu.VMEM((4, videos, 128), F32),
            pltpu.VMEM((videos, channels), F32),
            pltpu.VMEM((videos, channels), F32),
            pltpu.VMEM((videos, places, channels), BF16),
            pltpu.VMEM((videos, places, channels), BF16),
            pltpu.VMEM((2, loads, 2, places, channels), BF16),
            pltpu.VMEM((loads, 2, places, channels), BF16),
            pltpu.VMEM((loads, 2, places, channels), BF16),
            pltpu.VMEM((8, 128), jnp.int32),
            pltpu.VMEM((loads, 8, 128), jnp.int32),
            pltpu.SMEM((videos // 2,), jnp.int32),
            pltpu.SemaphoreType.DMA((12,)),
            pltpu.SemaphoreType.DMA((4,)),
            pltpu.SemaphoreType.DMA((videos // group,)),
            pltpu.SemaphoreType.DMA((videos // group,)),
            pltpu.SemaphoreType.DMA((3,)),
            pltpu.SemaphoreType.DMA((3,)),
            pltpu.SemaphoreType.DMA((spans // 4 - 1,)),
            pltpu.SemaphoreType.DMA((spans // 4 - 1,)),
            pltpu.SemaphoreType.DMA((3,)),
            pltpu.SemaphoreType.DMA((3,)),
            pltpu.SemaphoreType.DMA((2,)),
            pltpu.SemaphoreType.DMA((2,)),
        ],
        compiler_params=pltpu.CompilerParams(
            collective_id=0, has_side_effects=True, vmem_limit_bytes=63 * 1024 * 1024
        ),
    )(
        counts,
        dest.reshape(1, videos),
        frames[0],
        first_weight.reshape(3 * channels, channels),
        second_weight.reshape(3 * channels, channels),
        gain.reshape(1, channels),
        bias.reshape(1, channels),
    )
    return result[None]


def solution(mesh):
    loads, spans = mesh.shape["load"], mesh.shape["tm"]
    return jax.shard_map(
        functools.partial(body, loads, spans),
        mesh=mesh,
        in_specs=(
            P("tm", "load", None, None, None),
            P("tm", "load"),
            P("load"),
            P(),
            P(),
            P(),
            P(),
        ),
        out_specs=P("tm", "load", None, None, None),
        check_vma=False,
    )
```

time: 84.2 us -> 74.3 us (0.88)
  the two profiles are of different devices: /device:TPU:4 before, /device:TPU:1 now
where the time goes in v2:
time: 74.3 us; the launch traced here: 74.1 us
  Pallas kernels  72.1 us (97%)
  local copies, waits for them, and re-layouts  2.06 us (3%)
    pallas_call x1, Pallas kernels, body(): pl.pallas_call(functools.partial(kernel, loads, spans, group), out_shape=...  72.1 us
    unnamed x1, local copies, waits for them, and re-layouts  2.06 us

profile of v2, /device:TPU:1, one launch (start us, length us, event | category | flops | bytes accessed | tf_op | source)
XLA Modules:
  0.0 74.1 jit_solution(12076884334934320302)
XLA Ops:
  0.0 72.1 %shard_map.73 = bf16[32,2,24,256]{3,2,1,0:T(8,128)(2,1)} custom-call(s32[1,32]{1,0:T(1,128)} %counts_hbm.1, s32[1,32]{1,0:T(1,128)} %bitcast.13, bf16[32,8,24,256]{3,2,1,0:T(8,128)(2,1)} %bitcast.8, bf16[768,256]{1,0:T(8,128)(2,1)} %bitcast.9, bf16[768,256]{1,0:T(8,128)(2,1)} %bitcast.10, f32[1,256]{1,0:T(1,128)} %bitcast.11, f32[1,256]{1,0:T(1,128)} %bitcast.12), custom_call_target="tpu_custom_call" | custom-call | tf_op jit(solution)/shard_map/pallas_call | solution.py:403
  72.1 2.1 %copy.9 = bf16[1,32,2,24,256]{4,3,2,1,0:T(8,128)(2,1)} copy(bf16[1,32,2,24,256]{4,3,2,1,0:T(8,128)(2,1)} %bitcast.7) | data formatting | bytes 1572864

commit v3 on v2

--- a/solution.py
+++ b/solution.py
@@ -78,8 +78,8 @@
     sem_c_recv,
     sem_a_send,
     sem_a_recv,
-    sem_b_send,
-    sem_b_recv,
+    sem_ready,
+    sem_b,
     sem_s_send,
     sem_s_recv,
     sem_x_send,
@@ -87,7 +87,6 @@
 ):
     videos, places, channels = frames.shape[0], frames.shape[2], frames.shape[3]
     length = frames.shape[1]
-    teams = spans // 4
     quarter = channels // 4
     rows = group * places
     pairs = videos // 2
@@ -97,7 +96,9 @@
     seat = t % 4
     after = lax.rem(t + 1, spans)
     beyond = lax.rem(t + jnp.where(seat == 0, spans - 1, 1), spans)
-    edge = jnp.logical_or(seat == 0, seat == 3)
+    has_before, has_after = t > 0, t < spans - 1
+    team_before, team_after = t >= 4, t < spans - 4
+    edge = jnp.logical_or(jnp.logical_and(seat == 0, has_before), jnp.logical_and(seat == 3, has_after))
 
     pieces = 4
     part = videos // pieces
@@ -125,8 +126,10 @@
 
     for s in range(1, 4):
         greet(me, team * 4 + lax.rem(seat + s, 4))
-    for s in range(1, teams):
-        greet(me, lax.rem(team + s, teams) * 4 + seat)
+
+    @pl.when(team_after)
+    def _():
+        greet(me, lax.rem(t + 4, spans))
 
     @pl.loop(1, loads)
     def _(s):
@@ -150,7 +153,13 @@
     row = jnp.pad(dest_v[...], ((0, 7), (0, lanes - videos)), constant_values=-1)
     d_send[...] = row
 
-    pl.semaphore_wait(barrier, 3 + (teams - 1) + (loads - 1) + jnp.where(edge, 1, 0))
+    pl.semaphore_wait(barrier, 3 + (loads - 1) + jnp.where(edge, 1, 0) + jnp.where(team_before, 1, 0))
+
+    @pl.when(team_before)
+    def _():
+        pl.semaphore_signal(
+            sem_ready, inc=1, device_id=(me, lax.rem(t + spans - 4, spans)), device_id_type=MESH
+        )
 
     def remote(src, dst, ss, rs, load, place):
         return pltpu.make_async_remote_copy(
@@ -161,8 +170,10 @@
         place = pl.ds(pl.multiple_of(g * rows, rows), rows)
         return remote(t1_send.at[place], t1_recv.at[place], sem_c_send.at[g], sem_c_recv.at[g], me, after)
 
-    for g in range(videos // group):
-        context(g).start()
+    @pl.when(has_after)
+    def _():
+        for g in range(videos // group):
+            context(g).start()
 
     d_recv[me] = row
 
@@ -225,8 +236,12 @@
     def _(g):
         at = pl.ds(g * group, group)
         place = pl.ds(pl.multiple_of(g * rows, rows), rows)
-        context(g).wait_recv()
-        part = jnp.where(t > 0, t1_recv[place].astype(F32), 0.0)
+
+        @pl.when(has_before)
+        def _():
+            context(g).wait_recv()
+
+        part = jnp.where(has_before, t1_recv[place].astype(F32), 0.0)
         value = silu(part + dot(flat(frames[at, 0]), w1[2 * channels :])).astype(BF16)
         first[0, place] = value
         add_sums(g, at, value.astype(F32), False)
@@ -265,24 +280,19 @@
     totals = [a_recv[0]]
     for r in range(1, 4):
         totals.append(totals[-1] + a_recv[r])
-    b_send[...] = totals[-1]
-    b_copies = [
-        remote(
-            b_send,
-            b_recv.at[s - 1],
-            sem_b_send.at[s - 1],
-            sem_b_recv.at[s - 1],
-            me,
-            lax.rem(team + s, teams) * 4 + seat,
-        )
-        for s in range(1, teams)
-    ]
-    for copy in b_copies:
-        copy.start()
-    base = jnp.zeros_like(totals[0])
-    for s, copy in enumerate(b_copies, 1):
-        copy.wait_recv()
-        base = base + jnp.where(team >= s, b_recv[s - 1], 0.0)
+    b_copy = remote(b_send, b_recv, sem_b.at[0], sem_b.at[1], me, lax.rem(t + 4, spans))
+
+    @pl.when(team_before)
+    def _():
+        b_copy.wait_recv()
+
+    base = jnp.where(team_before, b_recv[...], 0.0)
+    b_send[...] = base + totals[-1]
+
+    @pl.when(team_after)
+    def _():
+        pl.semaphore_wait(sem_ready, 1)
+        b_copy.start()
 
     in_low = lax.broadcasted_iota(jnp.int32, (videos, lanes), 1) < quarter
     for r in range(4):
@@ -357,14 +367,21 @@
         t2_send[place] = dot(jnp.concatenate(ends, axis=1), w2[: 2 * channels]).astype(BF16)
 
     t2 = remote(t2_send, t2_recv, sem_t.at[0], sem_t.at[1], me, after)
-    t2.start()
-    t2.wait_recv()
+
+    @pl.when(has_after)
+    def _():
+        t2.start()
+
+
+    @pl.when(has_before)
+    def _():
+        t2.wait_recv()
 
     @pl.loop(0, videos // group)
     def _(g):
         at = pl.ds(g * group, group)
         place = pl.ds(pl.multiple_of(g * rows, rows), rows)
-        part = jnp.where(t > 0, t2_recv[place].astype(F32), 0.0)
+        part = jnp.where(has_before, t2_recv[place].astype(F32), 0.0)
         value = part + dot(first[0, place], w2[2 * channels :]) + bias[...]
         enc_0[at] = value.reshape(group, places, channels).astype(BF16)
 
@@ -377,10 +394,19 @@
     for i in range(pairs):
         table[i] = jnp.clip(jnp.sum(jnp.where(known == me * videos + 2 * i, loader, 0)), 0, loads - 1)
 
-    for g in range(videos // group):
-        context(g).wait_send()
-    for copy in [t2] + a_copies + b_copies + c_copies:
+    for copy in a_copies + c_copies:
         copy.wait_send()
+
+    @pl.when(has_after)
+    def _():
+        for g in range(videos // group):
+            context(g).wait_send()
+        t2.wait_send()
+
+    @pl.when(team_after)
+    def _():
+        b_copy.wait_send()
+
 
     for i in (1, 0):
         all_of(i).wait_recv()
@@ -427,7 +453,7 @@
             pltpu.VMEM((4,) + message, F32),
             pltpu.VMEM((4,) + message, F32),
             pltpu.VMEM(message, F32),
-            pltpu.VMEM((spans // 4 - 1,) + message, F32),
+            pltpu.VMEM(message, F32),
             pltpu.VMEM((4, videos, 128), F32),
             pltpu.VMEM((4, videos, 128), F32),
             pltpu.VMEM((videos, channels), F32),
@@ -446,8 +472,8 @@
             pltpu.SemaphoreType.DMA((videos // group,)),
             pltpu.SemaphoreType.DMA((3,)),
             pltpu.SemaphoreType.DMA((3,)),
-            pltpu.SemaphoreType.DMA((spans // 4 - 1,)),
-            pltpu.SemaphoreType.DMA((spans // 4 - 1,)),
+            pltpu.SemaphoreType.REGULAR,
+            pltpu.SemaphoreType.DMA((2,)),
             pltpu.SemaphoreType.DMA((3,)),
             pltpu.SemaphoreType.DMA((3,)),
             pltpu.SemaphoreType.DMA((2,)),

time: 74.3 us -> 63.9 us (0.86)
  the two profiles are of different devices: /device:TPU:1 before, /device:TPU:448 now
where the time goes in v3:
time: 63.9 us; the launch traced here: 63.7 us
  Pallas kernels  61.6 us (96%)
  local copies, waits for them, and re-layouts  2.06 us (3%)
    pallas_call x1, Pallas kernels, body(): pl.pallas_call(functools.partial(kernel, loads, spans, group), out_shape=...  61.6 us
    unnamed x1, local copies, waits for them, and re-layouts  2.06 us

profile of v3, /device:TPU:448, one launch (start us, length us, event | category | flops | bytes accessed | tf_op | source)
XLA Modules:
  0.0 63.7 jit_solution(15487911093644425947)
XLA Ops:
  0.0 61.6 %shard_map.73 = bf16[32,2,24,256]{3,2,1,0:T(8,128)(2,1)} custom-call(s32[1,32]{1,0:T(1,128)} %counts_hbm.1, s32[1,32]{1,0:T(1,128)} %bitcast.13, bf16[32,8,24,256]{3,2,1,0:T(8,128)(2,1)} %bitcast.8, bf16[768,256]{1,0:T(8,128)(2,1)} %bitcast.9, bf16[768,256]{1,0:T(8,128)(2,1)} %bitcast.10, f32[1,256]{1,0:T(1,128)} %bitcast.11, f32[1,256]{1,0:T(1,128)} %bitcast.12), custom_call_target="tpu_custom_call" | custom-call | tf_op jit(solution)/shard_map/pallas_call | solution.py:429
  61.6 2.1 %copy.9 = bf16[1,32,2,24,256]{4,3,2,1,0:T(8,128)(2,1)} copy(bf16[1,32,2,24,256]{4,3,2,1,0:T(8,128)(2,1)} %bitcast.7) | data formatting | bytes 1572864

commit v4 on v3

--- a/solution.py
+++ b/solution.py
@@ -138,17 +138,6 @@
     for fetch in fetches[:-3]:
         fetch.wait()
 
-    @pl.loop(0, videos)
-    def _(v):
-        tail[0, v] = frames[v, jnp.clip(cnt_s[0, v] - 2, 0, length - 1)]
-        tail[1, v] = frames[v, jnp.clip(cnt_s[0, v] - 1, 0, length - 1)]
-
-    @pl.loop(0, videos // group)
-    def _(g):
-        at = pl.ds(g * group, group)
-        lhs = jnp.concatenate([flat(tail[0, at]), flat(tail[1, at])], axis=1)
-        t1_send[pl.ds(pl.multiple_of(g * rows, rows), rows)] = dot(lhs, w1[: 2 * channels]).astype(BF16)
-
     lanes = 128
     row = jnp.pad(dest_v[...], ((0, 7), (0, lanes - videos)), constant_values=-1)
     d_send[...] = row
@@ -166,14 +155,26 @@
             src_ref=src, dst_ref=dst, send_sem=ss, recv_sem=rs, device_id=(load, place), device_id_type=MESH
         )
 
-    def context(g):
-        place = pl.ds(pl.multiple_of(g * rows, rows), rows)
-        return remote(t1_send.at[place], t1_recv.at[place], sem_c_send.at[g], sem_c_recv.at[g], me, after)
-
-    @pl.when(has_after)
-    def _():
-        for g in range(videos // group):
-            context(g).start()
+    few = min(8, videos)
+    few_rows = few * places
+
+    def context(q):
+        place = pl.ds(pl.multiple_of(q * few_rows, few_rows), few_rows)
+        return remote(t1_send.at[place], t1_recv.at[place], sem_c_send.at[q], sem_c_recv.at[q], me, after)
+
+    @pl.loop(0, videos // few)
+    def _(q):
+        for i in range(few):
+            v = q * few + i
+            tail[0, v] = frames[v, jnp.clip(cnt_s[0, v] - 2, 0, length - 1)]
+            tail[1, v] = frames[v, jnp.clip(cnt_s[0, v] - 1, 0, length - 1)]
+        at = pl.ds(q * few, few)
+        lhs = jnp.concatenate([flat(tail[0, at]), flat(tail[1, at])], axis=1)
+        t1_send[pl.ds(pl.multiple_of(q * few_rows, few_rows), few_rows)] = dot(lhs, w1[: 2 * channels]).astype(BF16)
+
+        @pl.when(has_after)
+        def _():
+            context(q).start()
 
     d_recv[me] = row
 
@@ -186,16 +187,8 @@
         fetch.wait()
     counts_row = cnt_v[...]
 
-    place_of = column(dest_v[...])
-    place_of = place_of // videos * 2 + place_of % 2
-    lane = lax.broadcasted_iota(jnp.int32, (videos, 128), 1)
-    video = lax.broadcasted_iota(jnp.int32, (videos, 128), 0)
-    pack_v[...] = jnp.clip(jnp.sum(jnp.where(place_of == lane, video, 0), axis=0, keepdims=True), 0, videos - 1)
-    to_scalars = pltpu.make_async_copy(pack_v, pack_s, sem_in.at[len(fetches)])
-    to_scalars.start()
-
-    def add_sums(g, at, values, fresh):
-        tiles = values.reshape(group, places // 8, 8, channels)
+    def add_sums(at, values, fresh):
+        tiles = values.reshape(-1, places // 8, 8, channels)
         s1 = jnp.sum(tiles, axis=1)
         s2 = jnp.sum(tiles * tiles, axis=1)
         if fresh:
@@ -224,27 +217,21 @@
             value = masked(silu(dot(lhs, w1[...])), group_live(g, 2 * j, lambda n: n))
             value = value.reshape(rows, channels).astype(BF16)
             first[j, place] = value
-            add_sums(g, at, value.astype(F32), j == 1)
-
-    @pl.loop(1, loads)
-    def _(s):
-        remote(d_send, d_recv.at[me], sem_t.at[2], sem_t.at[3], lax.rem(me + s, loads), t).start()
-
-    to_scalars.wait()
-
-    @pl.loop(0, videos // group)
-    def _(g):
-        at = pl.ds(g * group, group)
-        place = pl.ds(pl.multiple_of(g * rows, rows), rows)
+            add_sums(at, value.astype(F32), j == 1)
+
+    @pl.loop(0, videos // few)
+    def _(q):
+        at = pl.ds(q * few, few)
+        place = pl.ds(pl.multiple_of(q * few_rows, few_rows), few_rows)
 
         @pl.when(has_before)
         def _():
-            context(g).wait_recv()
+            context(q).wait_recv()
 
         part = jnp.where(has_before, t1_recv[place].astype(F32), 0.0)
         value = silu(part + dot(flat(frames[at, 0]), w1[2 * channels :])).astype(BF16)
         first[0, place] = value
-        add_sums(g, at, value.astype(F32), False)
+        add_sums(at, value.astype(F32), False)
 
     s1 = jnp.sum(acc1[...], axis=1)
     s2 = jnp.sum(acc2[...], axis=1)
@@ -270,6 +257,15 @@
     for copy in a_copies:
         copy.start()
     a_recv[seat] = a_send[seat]
+
+    place_of = column(dest_v[...])
+    place_of = place_of // videos * 2 + place_of % 2
+    lane = lax.broadcasted_iota(jnp.int32, (videos, 128), 1)
+    video = lax.broadcasted_iota(jnp.int32, (videos, 128), 0)
+    pack_v[...] = jnp.clip(jnp.sum(jnp.where(place_of == lane, video, 0), axis=0, keepdims=True), 0, videos - 1)
+    to_scalars = pltpu.make_async_copy(pack_v, pack_s, sem_in.at[len(fetches)])
+    to_scalars.start()
+
     my_gain = sum(jnp.where(seat == r, g, 0.0) for r, g in enumerate(parts(gain[...])))
     my_gain = jnp.concatenate([my_gain, my_gain], axis=1)
     for s in range(1, 4):
@@ -336,21 +332,28 @@
         mean = mean_v[at][:, None, :]
         scale = scale_v[at][:, None, :]
         taps = []
-        for j in range(4):
+        for j in range(3):
             value = first[j, place].astype(F32).reshape(group, places, channels)
             value = ((value - mean) * scale).reshape(rows, channels).astype(BF16)
             first[j, place] = value
             taps.append(value)
-        lhs = jnp.concatenate(taps[:3], axis=1)
+        lhs = jnp.concatenate(taps, axis=1)
         value = masked(dot(lhs, w2[...]) + bias[...], group_live(g, 2, lambda n: (n + 1) // 2))
         enc_1[at] = value.astype(BF16)
 
+    to_scalars.wait()
     exchange(1)
+
+    @pl.loop(1, loads)
+    def _(s):
+        remote(d_send, d_recv.at[me], sem_t.at[2], sem_t.at[3], lax.rem(me + s, loads), t).start()
 
     @pl.loop(0, videos // group)
     def _(g):
         place = pl.ds(pl.multiple_of(g * rows, rows), rows)
+        at = pl.ds(pl.multiple_of(g * group, group), group)
         normed = [first[j, place].astype(F32).reshape(group, places, channels) for j in range(4)]
+        normed[3] = (normed[3] - mean_v[at][:, None, :]) * scale_v[at][:, None, :]
         ends = []
         for k in range(2):
             pieces = []
@@ -399,8 +402,8 @@
 
     @pl.when(has_after)
     def _():
-        for g in range(videos // group):
-            context(g).wait_send()
+        for q in range(videos // few):
+            context(q).wait_send()
         t2.wait_send()
 
     @pl.when(team_after)
@@ -468,8 +471,8 @@
             pltpu.SMEM((videos // 2,), jnp.int32),
             pltpu.SemaphoreType.DMA((12,)),
             pltpu.SemaphoreType.DMA((4,)),
-            pltpu.SemaphoreType.DMA((videos // group,)),
-            pltpu.SemaphoreType.DMA((videos // group,)),
+            pltpu.SemaphoreType.DMA((videos // min(8, videos),)),
+            pltpu.SemaphoreType.DMA((videos // min(8, videos),)),
             pltpu.SemaphoreType.DMA((3,)),
             pltpu.SemaphoreType.DMA((3,)),
             pltpu.SemaphoreType.REGULAR,

time: 63.9 us -> 67.3 us (1.053)
  Pallas kernels: 61.6 us -> 64.4 us
    pallas_call x1, Pallas kernels: 61.6 us -> 64.4 us  [body(): pl.pallas_call(functools.partial(kernel, loads, spans, group), out_shape=...]
where the time goes in v4:
time: 67.3 us; the launch traced here: 66.5 us
  Pallas kernels  64.4 us (96%)
  local copies, waits for them, and re-layouts  2.06 us (3%)
    pallas_call x1, Pallas kernels, body(): pl.pallas_call(functools.partial(kernel, loads, spans, group), out_shape=...  64.4 us
    unnamed x1, local copies, waits for them, and re-layouts  2.06 us

profile of v4, /device:TPU:448, one launch (start us, length us, event | category | flops | bytes accessed | tf_op | source)
XLA Modules:
  0.0 66.5 jit_solution(7265869489815313991)
XLA Ops:
  0.0 64.4 %shard_map.73 = bf16[32,2,24,256]{3,2,1,0:T(8,128)(2,1)} custom-call(s32[1,32]{1,0:T(1,128)} %counts_hbm.1, s32[1,32]{1,0:T(1,128)} %bitcast.13, bf16[32,8,24,256]{3,2,1,0:T(8,128)(2,1)} %bitcast.8, bf16[768,256]{1,0:T(8,128)(2,1)} %bitcast.9, bf16[768,256]{1,0:T(8,128)(2,1)} %bitcast.10, f32[1,256]{1,0:T(1,128)} %bitcast.11, f32[1,256]{1,0:T(1,128)} %bitcast.12), custom_call_target="tpu_custom_call" | custom-call | tf_op jit(solution)/shard_map/pallas_call | solution.py:432
  64.5 2.1 %copy.9 = bf16[1,32,2,24,256]{4,3,2,1,0:T(8,128)(2,1)} copy(bf16[1,32,2,24,256]{4,3,2,1,0:T(8,128)(2,1)} %bitcast.7) | data formatting | bytes 1572864

commit v5 on v3

--- a/solution.py
+++ b/solution.py
@@ -186,14 +186,6 @@
         fetch.wait()
     counts_row = cnt_v[...]
 
-    place_of = column(dest_v[...])
-    place_of = place_of // videos * 2 + place_of % 2
-    lane = lax.broadcasted_iota(jnp.int32, (videos, 128), 1)
-    video = lax.broadcasted_iota(jnp.int32, (videos, 128), 0)
-    pack_v[...] = jnp.clip(jnp.sum(jnp.where(place_of == lane, video, 0), axis=0, keepdims=True), 0, videos - 1)
-    to_scalars = pltpu.make_async_copy(pack_v, pack_s, sem_in.at[len(fetches)])
-    to_scalars.start()
-
     def add_sums(g, at, values, fresh):
         tiles = values.reshape(group, places // 8, 8, channels)
         s1 = jnp.sum(tiles, axis=1)
@@ -230,8 +222,6 @@
     def _(s):
         remote(d_send, d_recv.at[me], sem_t.at[2], sem_t.at[3], lax.rem(me + s, loads), t).start()
 
-    to_scalars.wait()
-
     @pl.loop(0, videos // group)
     def _(g):
         at = pl.ds(g * group, group)
@@ -270,6 +260,15 @@
     for copy in a_copies:
         copy.start()
     a_recv[seat] = a_send[seat]
+
+    place_of = column(dest_v[...])
+    place_of = place_of // videos * 2 + place_of % 2
+    lane = lax.broadcasted_iota(jnp.int32, (videos, 128), 1)
+    video = lax.broadcasted_iota(jnp.int32, (videos, 128), 0)
+    pack_v[...] = jnp.clip(jnp.sum(jnp.where(place_of == lane, video, 0), axis=0, keepdims=True), 0, videos - 1)
+    to_scalars = pltpu.make_async_copy(pack_v, pack_s, sem_in.at[len(fetches)])
+    to_scalars.start()
+
     my_gain = sum(jnp.where(seat == r, g, 0.0) for r, g in enumerate(parts(gain[...])))
     my_gain = jnp.concatenate([my_gain, my_gain], axis=1)
     for s in range(1, 4):
@@ -336,21 +335,24 @@
         mean = mean_v[at][:, None, :]
         scale = scale_v[at][:, None, :]
         taps = []
-        for j in range(4):
+        for j in range(3):
             value = first[j, place].astype(F32).reshape(group, places, channels)
             value = ((value - mean) * scale).reshape(rows, channels).astype(BF16)
             first[j, place] = value
             taps.append(value)
-        lhs = jnp.concatenate(taps[:3], axis=1)
+        lhs = jnp.concatenate(taps, axis=1)
         value = masked(dot(lhs, w2[...]) + bias[...], group_live(g, 2, lambda n: (n + 1) // 2))
         enc_1[at] = value.astype(BF16)
 
+    to_scalars.wait()
     exchange(1)
 
     @pl.loop(0, videos // group)
     def _(g):
         place = pl.ds(pl.multiple_of(g * rows, rows), rows)
+        at = pl.ds(pl.multiple_of(g * group, group), group)
         normed = [first[j, place].astype(F32).reshape(group, places, channels) for j in range(4)]
+        normed[3] = (normed[3] - mean_v[at][:, None, :]) * scale_v[at][:, None, :]
         ends = []
         for k in range(2):
             pieces = []
@@ -480,16 +482,21 @@
             pltpu.SemaphoreType.DMA((2,)),
         ],
         compiler_params=pltpu.CompilerParams(
-            collective_id=0, has_side_effects=True, vmem_limit_bytes=63 * 1024 * 1024
+            collective_id=0, has_side_effects=True, vmem_limit_bytes=48 * 1024 * 1024
         ),
     )(
-        counts,
-        dest.reshape(1, videos),
-        frames[0],
-        first_weight.reshape(3 * channels, channels),
-        second_weight.reshape(3 * channels, channels),
-        gain.reshape(1, channels),
-        bias.reshape(1, channels),
+        *(
+            pltpu.with_memory_space_constraint(operand, pltpu.HBM)
+            for operand in (
+                counts,
+                dest.reshape(1, videos),
+                frames[0],
+                first_weight.reshape(3 * channels, channels),
+                second_weight.reshape(3 * channels, channels),
+                gain.reshape(1, channels),
+                bias.reshape(1, channels),
+            )
+        )
     )
     return result[None]
 

time: 63.9 us -> 61.7 us (0.966)
  local copies, waits for them, and re-layouts: 2.06 us -> 0.88 us
  Pallas kernels: 61.6 us -> 60.7 us
    unnamed x1, local copies, waits for them, and re-layouts: 2.06 us -> 0.88 us
    pallas_call x1, Pallas kernels: 61.6 us -> 60.7 us  [body(): pl.pallas_call(functools.partial(kernel, loads, spans, group), out_shape=...]
where the time goes in v5:
time: 61.7 us; the launch traced here: 61.6 us
  Pallas kernels  60.7 us (98%)
  local copies, waits for them, and re-layouts  0.88 us (1%)
    pallas_call x1, Pallas kernels, body(): pl.pallas_call(functools.partial(kernel, loads, spans, group), out_shape=...  60.7 us

profile of v5, /device:TPU:448, one launch (start us, length us, event | category | flops | bytes accessed | tf_op | source)
XLA Modules:
  0.0 61.6 jit_solution(2228951431705802094)
XLA Ops:
  0.0 60.7 %shard_map.73 = bf16[32,2,24,256]{3,2,1,0:T(8,128)(2,1)S(1)} custom-call(s32[1,32]{1,0:T(1,128)} %counts_hbm.1, s32[1,32]{1,0:T(1,128)} %bitcast.13, bf16[32,8,24,256]{3,2,1,0:T(8,128)(2,1)} %bitcast.8, bf16[768,256]{1,0:T(8,128)(2,1)} %bitcast.9, bf16[768,256]{1,0:T(8,128)(2,1)} %bitcast.10, f32[1,256]{1,0:T(1,128)} %bitcast.11, f32[1,256]{1,0:T(1,128)} %bitcast.12), custom_call_target="tpu_custom_call" | custom-call | tf_op jit(solution)/shard_map/pallas_call | solution.py:431
  60.7 0.9 %copy.9 = bf16[1,32,2,24,256]{4,3,2,1,0:T(8,128)(2,1)} copy(bf16[1,32,2,24,256]{4,3,2,1,0:T(8,128)(2,1)S(1)} %bitcast.7) | data formatting | bytes 1572864

commit v6 on v5

--- a/solution.py
+++ b/solution.py
@@ -97,7 +97,7 @@
     after = lax.rem(t + 1, spans)
     beyond = lax.rem(t + jnp.where(seat == 0, spans - 1, 1), spans)
     has_before, has_after = t > 0, t < spans - 1
-    team_before, team_after = t >= 4, t < spans - 4
+    teams = spans // 4
     edge = jnp.logical_or(jnp.logical_and(seat == 0, has_before), jnp.logical_and(seat == 3, has_after))
 
     pieces = 4
@@ -127,9 +127,11 @@
     for s in range(1, 4):
         greet(me, team * 4 + lax.rem(seat + s, 4))
 
-    @pl.when(team_after)
-    def _():
-        greet(me, lax.rem(t + 4, spans))
+    for s in range(1, teams):
+
+        @pl.when(team + s < teams)
+        def _():
+            greet(me, lax.rem(t + 4 * s, spans))
 
     @pl.loop(1, loads)
     def _(s):
@@ -153,13 +155,18 @@
     row = jnp.pad(dest_v[...], ((0, 7), (0, lanes - videos)), constant_values=-1)
     d_send[...] = row
 
-    pl.semaphore_wait(barrier, 3 + (loads - 1) + jnp.where(edge, 1, 0) + jnp.where(team_before, 1, 0))
-
-    @pl.when(team_before)
-    def _():
-        pl.semaphore_signal(
-            sem_ready, inc=1, device_id=(me, lax.rem(t + spans - 4, spans)), device_id_type=MESH
-        )
+    pl.semaphore_wait(barrier, 3 + (loads - 1) + jnp.where(edge, 1, 0) + team)
+
+    for s in range(1, teams):
+
+        @pl.when(team >= s)
+        def _():
+            pl.semaphore_signal(
+                sem_ready.at[s - 1],
+                inc=1,
+                device_id=(me, lax.rem(t + spans - 4 * s, spans)),
+                device_id_type=MESH,
+            )
 
     def remote(src, dst, ss, rs, load, place):
         return pltpu.make_async_remote_copy(
@@ -279,19 +286,27 @@
     totals = [a_recv[0]]
     for r in range(1, 4):
         totals.append(totals[-1] + a_recv[r])
-    b_copy = remote(b_send, b_recv, sem_b.at[0], sem_b.at[1], me, lax.rem(t + 4, spans))
-
-    @pl.when(team_before)
-    def _():
-        b_copy.wait_recv()
-
-    base = jnp.where(team_before, b_recv[...], 0.0)
-    b_send[...] = base + totals[-1]
-
-    @pl.when(team_after)
-    def _():
-        pl.semaphore_wait(sem_ready, 1)
-        b_copy.start()
+    def totals_to(s):
+        return remote(
+            b_send, b_recv.at[s - 1], sem_b.at[0, s - 1], sem_b.at[1, s - 1], me, lax.rem(t + 4 * s, spans)
+        )
+
+    b_send[...] = totals[-1]
+    for s in range(1, teams):
+
+        @pl.when(team + s < teams)
+        def _():
+            pl.semaphore_wait(sem_ready.at[s - 1], 1)
+            totals_to(s).start()
+
+    base = jnp.zeros_like(totals[0])
+    for s in range(teams - 1, 0, -1):
+
+        @pl.when(team >= s)
+        def _():
+            totals_to(s).wait_recv()
+
+        base = base + jnp.where(team >= s, b_recv[s - 1], 0.0)
 
     in_low = lax.broadcasted_iota(jnp.int32, (videos, lanes), 1) < quarter
     for r in range(4):
@@ -405,9 +420,11 @@
             context(g).wait_send()
         t2.wait_send()
 
-    @pl.when(team_after)
-    def _():
-        b_copy.wait_send()
+    for s in range(1, teams):
+
+        @pl.when(team + s < teams)
+        def _():
+            totals_to(s).wait_send()
 
 
     for i in (1, 0):
@@ -455,7 +472,7 @@
             pltpu.VMEM((4,) + message, F32),
             pltpu.VMEM((4,) + message, F32),
             pltpu.VMEM(message, F32),
-            pltpu.VMEM(message, F32),
+            pltpu.VMEM((spans // 4 - 1,) + message, F32),
             pltpu.VMEM((4, videos, 128), F32),
             pltpu.VMEM((4, videos, 128), F32),
             pltpu.VMEM((videos, channels), F32),
@@ -474,8 +491,8 @@
             pltpu.SemaphoreType.DMA((videos // group,)),
             pltpu.SemaphoreType.DMA((3,)),
             pltpu.SemaphoreType.DMA((3,)),
-            pltpu.SemaphoreType.REGULAR,
-            pltpu.SemaphoreType.DMA((2,)),
+            pltpu.SemaphoreType.REGULAR((spans // 4 - 1,)),
+            pltpu.SemaphoreType.DMA((2, spans // 4 - 1)),
             pltpu.SemaphoreType.DMA((3,)),
             pltpu.SemaphoreType.DMA((3,)),
             pltpu.SemaphoreType.DMA((2,)),

time: 61.7 us -> 60.7 us (0.984)
  Pallas kernels: 60.7 us -> 59.7 us
    pallas_call x1, Pallas kernels: 60.7 us -> 59.7 us  [body(): pl.pallas_call(functools.partial(kernel, loads, spans, group), out_shape=...]
where the time goes in v6:
time: 60.7 us; the launch traced here: 60.6 us
  Pallas kernels  59.7 us (98%)
  local copies, waits for them, and re-layouts  0.88 us (1%)
    pallas_call x1, Pallas kernels, body(): pl.pallas_call(functools.partial(kernel, loads, spans, group), out_shape=...  59.7 us

profile of v6, /device:TPU:448, one launch (start us, length us, event | category | flops | bytes accessed | tf_op | source)
XLA Modules:
  0.0 60.6 jit_solution(17734505569890443688)
XLA Ops:
  0.0 59.7 %shard_map.73 = bf16[32,2,24,256]{3,2,1,0:T(8,128)(2,1)S(1)} custom-call(s32[1,32]{1,0:T(1,128)} %counts_hbm.1, s32[1,32]{1,0:T(1,128)} %bitcast.13, bf16[32,8,24,256]{3,2,1,0:T(8,128)(2,1)} %bitcast.8, bf16[768,256]{1,0:T(8,128)(2,1)} %bitcast.9, bf16[768,256]{1,0:T(8,128)(2,1)} %bitcast.10, f32[1,256]{1,0:T(1,128)} %bitcast.11, f32[1,256]{1,0:T(1,128)} %bitcast.12), custom_call_target="tpu_custom_call" | custom-call | tf_op jit(solution)/shard_map/pallas_call | solution.py:448
  59.7 0.9 %copy.9 = bf16[1,32,2,24,256]{4,3,2,1,0:T(8,128)(2,1)} copy(bf16[1,32,2,24,256]{4,3,2,1,0:T(8,128)(2,1)S(1)} %bitcast.7) | data formatting | bytes 1572864

commit v7 on v6

--- a/solution.py
+++ b/solution.py
@@ -145,12 +145,12 @@
         tail[0, v] = frames[v, jnp.clip(cnt_s[0, v] - 2, 0, length - 1)]
         tail[1, v] = frames[v, jnp.clip(cnt_s[0, v] - 1, 0, length - 1)]
 
-    @pl.loop(0, videos // group)
-    def _(g):
+    def products(g):
         at = pl.ds(g * group, group)
         lhs = jnp.concatenate([flat(tail[0, at]), flat(tail[1, at])], axis=1)
-        t1_send[pl.ds(pl.multiple_of(g * rows, rows), rows)] = dot(lhs, w1[: 2 * channels]).astype(BF16)
-
+        t1_send[pl.ds(g * rows, rows)] = dot(lhs, w1[: 2 * channels]).astype(BF16)
+
+    products(0)
     lanes = 128
     row = jnp.pad(dest_v[...], ((0, 7), (0, lanes - videos)), constant_values=-1)
     d_send[...] = row
@@ -177,9 +177,12 @@
         place = pl.ds(pl.multiple_of(g * rows, rows), rows)
         return remote(t1_send.at[place], t1_recv.at[place], sem_c_send.at[g], sem_c_recv.at[g], me, after)
 
-    @pl.when(has_after)
-    def _():
-        for g in range(videos // group):
+    for g in range(videos // group):
+        if g > 0:
+            products(g)
+
+        @pl.when(has_after)
+        def _():
             context(g).start()
 
     d_recv[me] = row

time: 60.7 us -> 60.7 us (level)
  no operation moved by 1% of the time
where the time goes in v7:
time: 60.7 us; the launch traced here: 60.6 us
  Pallas kernels  59.7 us (98%)
  local copies, waits for them, and re-layouts  0.88 us (1%)
    pallas_call x1, Pallas kernels, body(): pl.pallas_call(functools.partial(kernel, loads, spans, group), out_shape=...  59.7 us

profile of v7, /device:TPU:448, one launch (start us, length us, event | category | flops | bytes accessed | tf_op | source)
XLA Modules:
  0.0 60.6 jit_solution(13882206143069034934)
XLA Ops:
  0.0 59.7 %shard_map.73 = bf16[32,2,24,256]{3,2,1,0:T(8,128)(2,1)S(1)} custom-call(s32[1,32]{1,0:T(1,128)} %counts_hbm.1, s32[1,32]{1,0:T(1,128)} %bitcast.13, bf16[32,8,24,256]{3,2,1,0:T(8,128)(2,1)} %bitcast.8, bf16[768,256]{1,0:T(8,128)(2,1)} %bitcast.9, bf16[768,256]{1,0:T(8,128)(2,1)} %bitcast.10, f32[1,256]{1,0:T(1,128)} %bitcast.11, f32[1,256]{1,0:T(1,128)} %bitcast.12), custom_call_target="tpu_custom_call" | custom-call | tf_op jit(solution)/shard_map/pallas_call | solution.py:451
  59.7 0.9 %copy.9 = bf16[1,32,2,24,256]{4,3,2,1,0:T(8,128)(2,1)} copy(bf16[1,32,2,24,256]{4,3,2,1,0:T(8,128)(2,1)S(1)} %bitcast.7) | data formatting | bytes 1572864
